TPU v7x, 32 devices: a whole 2x2x4 slice. The times are simulated.
32 devices in a mesh: req: 4 (over x, core), tp: 8 (over z, y).
Axes of the slice: x: 2, y: 2, z: 4, core: 2. Of those that a mesh axis runs over, the one named last changes fastest.
Arguments:
- hidden: bfloat16 [4, 320, 5120], P('req'), may hold values from -6 to 6
- norm_gain: float32 [5120], replicated, may hold values from 0.5 to 2
- q_weight: float32 [5120, 1024], P(('req', 'tp')), may hold values from -0.078125 to 0.078125
- k_weight: float32 [5120, 1024], P(('req', 'tp')), may hold values from -0.078125 to 0.078125
- v_weight: float32 [5120, 1024], P(('req', 'tp')), may hold values from -0.078125 to 0.078125
- o_weight: float32 [5120, 1024], P(('req', 'tp')), may hold values from -0.5 to 0.5
- key_cache: bfloat16 [4, 512, 1024], P('req', None, 'tp'), may hold values from -160 to 160
- value_cache: bfloat16 [4, 512, 1024], P('req', None, 'tp'), may hold values from -6 to 6
- text_rows: bfloat16 [4, 256, 5120], P('req', 'tp'), may hold values from -6 to 6
- text_index: int32 [4, 256], P('req'), may hold values from 0 to 511, as said below
- clip_len: int32 [4], P('req'), may hold values from 80 to 320, as said below
- text_len: int32 [4], P('req'), may hold values from 128 to 512, as said below
Outputs:
- output: bfloat16 [4, 320, 5120], P('req', 'tp')
Inputs may be any that keep to these rules, and one draw needn't show every extreme that they name: `text_index`: within a clip the entries are distinct text rows; clip 0 always recomputes rows 0 and 511. `clip_len`: some clip has exactly 320 live slots and some clip exactly 80. `text_len`: some clip has all 512 text rows live and some clip exactly 128.
All inputs are finite; a program needn't handle non-finite values.
Results may differ from a plain program's by a relative error of at most 0.012.
The roundings to bfloat16 on the way count: a program that leaves them out, or rounds other values in their place, can miss the bound.
Values may be sent and summed in bfloat16 or wider, within the bound.
A program may use at most 64 MiB of HBM per device.

v0:
```python
import math
import jax
import jax.numpy as jnp
from jax import lax
from jax.sharding import PartitionSpec as P


def on_device(
    hidden,
    norm_gain,
    q_weight,
    k_weight,
    v_weight,
    o_weight,
    key_cache,
    value_cache,
    text_rows,
    text_index,
    clip_len,
    text_len,
):
    head_width = key_cache.shape[2]
    text_total = key_cache.shape[1]
    q_half = q_weight.astype(jnp.bfloat16)
    k_half = k_weight.astype(jnp.bfloat16)
    v_half = v_weight.astype(jnp.bfloat16)
    o_half = o_weight.astype(jnp.bfloat16)
    q_block, k_block, v_block, o_block = (
        lax.all_to_all(q_half, "tp", split_axis=1, concat_axis=0, tiled=True),
        lax.all_to_all(k_half, "tp", split_axis=1, concat_axis=0, tiled=True),
        lax.all_to_all(v_half, "tp", split_axis=1, concat_axis=0, tiled=True),
        lax.all_to_all(o_half, "tp", split_axis=1, concat_axis=0, tiled=True),
    )
    q_local, k_local, v_local, o_local = (
        lax.all_gather(q_block, "req", axis=0, tiled=True),
        lax.all_gather(k_block, "req", axis=0, tiled=True),
        lax.all_gather(v_block, "req", axis=0, tiled=True),
        lax.all_gather(o_block, "req", axis=0, tiled=True),
    )
    x32 = hidden[0].astype(jnp.float32)
    mean = jnp.mean(x32, axis=-1, keepdims=True)
    centered = x32 - mean
    var = jnp.mean(centered * centered, axis=-1, keepdims=True)
    normed = (centered * lax.rsqrt(var + 1e-06) * norm_gain).astype(jnp.bfloat16)
    kv_local = jnp.concatenate([k_local, v_local], axis=1)
    new_kv = jnp.einsum(
        "crd,de->cre",
        lax.all_gather(text_rows, "tp", axis=1, tiled=True),
        kv_local,
        preferred_element_type=jnp.float32,
    ).astype(jnp.bfloat16)
    query = jnp.dot(normed, q_local, preferred_element_type=jnp.float32).astype(jnp.bfloat16)
    selector = text_index[0][None, :] == jnp.arange(text_total, dtype=jnp.int32)[:, None]
    covered = jnp.any(selector, axis=1)
    placed = jnp.dot(
        selector.astype(jnp.bfloat16), new_kv[0], preferred_element_type=jnp.float32
    ).astype(jnp.bfloat16)
    keys = jnp.where(covered[:, None], placed[:, :head_width], key_cache[0])
    values = jnp.where(covered[:, None], placed[:, head_width:], value_cache[0])
    score = lax.dot_general(
        query, keys, (((1,), (1,)), ((), ())), preferred_element_type=jnp.float32
    ) * (1.0 / math.sqrt(head_width))
    valid = jnp.arange(text_total, dtype=jnp.int32) < text_len[0]
    score = jnp.where(valid[None, :], score, -1e30)
    top = jnp.max(score, axis=-1, keepdims=True)
    expo = jnp.exp(score - top)
    weights = (expo / jnp.sum(expo, axis=-1, keepdims=True)).astype(jnp.bfloat16)
    attended = jnp.dot(weights, values, preferred_element_type=jnp.float32).astype(jnp.bfloat16)
    tp_count = lax.axis_size("tp")
    local_rows = hidden.shape[1] // tp_count
    first_row = lax.axis_index("tp") * local_rows
    summed = lax.psum_scatter(
        lax.dot_general(
            attended, o_local, (((1,), (1,)), ((), ())), preferred_element_type=jnp.float32
        ).astype(jnp.bfloat16),
        "tp",
        scatter_dimension=0,
        tiled=True,
    ).astype(jnp.float32)
    own_rows = lax.dynamic_slice_in_dim(x32, first_row, local_rows, 0)
    positions = first_row + jnp.arange(local_rows, dtype=jnp.int32)
    live = positions < clip_len[0]
    result = own_rows + jnp.where(live[:, None], summed, 0.0)
    return result.astype(jnp.bfloat16)[None]


def solution(mesh):
    return jax.shard_map(
        on_device,
        mesh=mesh,
        in_specs=(
            P("req", None, None),
            P(),
            P(("req", "tp"), None),
            P(("req", "tp"), None),
            P(("req", "tp"), None),
            P(("req", "tp"), None),
            P("req", None, "tp"),
            P("req", None, "tp"),
            P("req", "tp", None),
            P("req", None),
            P("req"),
            P("req"),
        ),
        out_specs=P("req", "tp", None),
        check_vma=False,
    )
```

profile of v0, /device:TPU:0, one launch (start us, length us, event | category | flops | bytes accessed | tf_op | source)
XLA Modules:
  0.0 247.2 jit_solution(8818809206935015885)
XLA Ops:
  6.5 1.1 copy_bitcast_fusion.2
  7.7 18.1 %all_to_all.76 = bf16[160,8,128]{2,0,1:T(8,128)(2,1)} all-to-all(bf16[160,8,128]{2,0,1:T(8,128)(2,1)S(1)} %copy_bitcast_fusion.2), channel_id=1, replica_groups=mesh['req'=4,'tp'=8] {'tp'}, dimensions={1} | all-to-all | bytes 655360 | tf_op jit(solution)/shard_map/all_to_all | solution.py:30
  25.8 1.3 copy_bitcast_fusion.1
  27.1 13.7 %all_to_all.77 = bf16[160,8,128]{2,0,1:T(8,128)(2,1)} all-to-all(bf16[160,8,128]{2,0,1:T(8,128)(2,1)S(1)} %copy_bitcast_fusion.1), channel_id=1, replica_groups=mesh['req'=4,'tp'=8] {'tp'}, dimensions={1} | all-to-all | bytes 655360 | tf_op jit(solution)/shard_map/all_to_all | solution.py:31
  40.9 0.7 all-gather.12.cloned.1.call-update
  41.7 1.1 copy_bitcast_fusion.3
  42.8 13.2 %all_to_all.78 = bf16[160,8,128]{2,0,1:T(8,128)(2,1)} all-to-all(bf16[160,8,128]{2,0,1:T(8,128)(2,1)S(1)} %copy_bitcast_fusion.3), channel_id=1, replica_groups=mesh['req'=4,'tp'=8] {'tp'}, dimensions={1} | all-to-all | bytes 655360 | tf_op jit(solution)/shard_map/all_to_all | solution.py:29
  56.1 1.9 copy_bitcast_fusion
  57.9 4.1 %all-to-all-start.3 = ((bf16[160,8,128]{2,0,1:T(8,128)(2,1)}), bf16[160,8,128]{2,0,1:T(8,128)(2,1)}, u32[]{:S(2)}, u32[]{:S(2)}) async-start(bf16[160,8,128]{2,0,1:T(8,128)(2,1)} %copy_bitcast_fusion), calls=%async_computation.3 | async-start | bytes 655360 | tf_op jit(solution)/shard_map/all_to_all | solution.py:32
  62.7 0.5 convert_reduce_fusion
  63.3 7.6 %all-to-all-done.3 = bf16[160,8,128]{2,0,1:T(8,128)(2,1)} async-done(((bf16[160,8,128]{2,0,1:T(8,128)(2,1)}), bf16[160,8,128]{2,0,1:T(8,128)(2,1)}, u32[]{:S(2)}, u32[]{:S(2)}) %all-to-all-start.3) | async-done | bytes 327712 | tf_op jit(solution)/shard_map/all_to_all | solution.py:32
  70.9 0.6 iota_compare_fusion.2
  71.5 0.2 fusion.22
  71.7 1.0 multiply_reduce_fusion
  72.8 46.5 %all-gather.12.cloned.1.call-done = bf16[1,256,5120]{2,1,0:T(8,128)(2,1)} async-done(((bf16[1,32,5120]{2,1,0:T(8,128)(2,1)}), bf16[1,256,5120]{2,1,0:T(8,128)(2,1)}) %all-gather.12.cloned.1.call-update) | async-done | bytes 2621456 | tf_op jit(solution)/shard_map/all_gather | solution.py:48
  119.2 4.4 %convolution_convert_fusion.1 = bf16[512,256]{1,0:T(8,128)(2,1)} fusion(bf16[1,256,5120]{2,1,0:T(8,128)(2,1)} %all-gather.12.cloned.1.call-done, bf16[5120,128]{1,0:T(8,128)(2,1)} %all-gather.10.cloned.1.call-done, bf16[5120,128]{1,0:T(8,128)(2,1)} %all-gather.8.cloned.1.call-done, s32[256]{0:T(256)S(1)} %bitcast.84), kind=kOutput, calls=%fused_computation.16 | convolution fusion | flops 743768064 | bytes 5506048 | tf_op jit(solution)/shard_map/dot_general | solution.py:55
  123.7 13.8 %all-gather.6.cloned.1.call-done = bf16[5120,128]{1,0:T(8,128)(2,1)} async-done(((bf16[1280,128]{1,0:T(8,128)(2,1)}), bf16[5120,128]{1,0:T(8,128)(2,1)}) %all-gather.6.cloned.1.call-update) | async-done | bytes 1310736 | tf_op jit(solution)/shard_map/all_gather | solution.py:35
  137.4 3.6 %fusion.37 = (f32[320]{0:T(512)S(1)}, f32[320,512]{1,0:T(8,128)}) fusion(bf16[512,256]{1,0:T(8,128)(2,1)} %convolution_convert_fusion.1, bf16[1,512,128]{2,1,0:T(8,128)(2,1)S(1)} %copy-done.2, pred[512]{0:T(512)(128)(4,1)S(1)} %fusion.22, bf16[5120,128]{1,0:T(8,128)(2,1)} %all-gather.6.cloned.1.call-done, bf16[1,320,5120]{2,1,0:T(8,128)(2,1)S(1)} %copy-done, ...), kind=kOutput, calls=%fused_computation.50 | convolution fusion | flops 470163136 | bytes 5530368 | tf_op jit(solution)/shard_map/dot_general | solution.py:60
  141.1 1.3 fusion.21
  142.4 14.7 %all-gather.14.cloned.1.call-done = bf16[5120,128]{1,0:T(8,128)(2,1)} async-done(((bf16[1280,128]{1,0:T(8,128)(2,1)}), bf16[5120,128]{1,0:T(8,128)(2,1)}) %all-gather.14.cloned.1.call-update) | async-done | bytes 1310736 | tf_op jit(solution)/shard_map/all_gather | solution.py:38
  157.1 4.8 %convolution_convert_fusion = bf16[320,5120]{1,0:T(8,128)(2,1)} fusion(bf16[5120,128]{1,0:T(8,128)(2,1)} %all-gather.14.cloned.1.call-done, f32[320,512]{1,0:T(8,128)} %get-tuple-element.6, f32[320]{0:T(512)S(1)} %fusion.21, f32[320]{0:T(512)S(1)} %get-tuple-element.5, bf16[512,256]{1,0:T(8,128)(2,1)} %convolution_convert_fusion.1, ...), kind=kOutput, calls=%fused_computation | convolution fusion | flops 463609856 | bytes 5508096 | tf_op jit(solution)/shard_map/dot_general | solution.py:73
  161.9 3.5 %convert_element_type.48 = f32[1,320,5120]{2,1,0:T(8,128)} convert(bf16[1,320,5120]{2,1,0:T(8,128)(2,1)S(1)} %copy-done) | non-fusion elementwise | flops 1638400 | bytes 9830400 | tf_op jit(solution)/shard_map/convert_element_type | solution.py:40
  166.0 72.1 %reduce-scatter.2.cloned.1.call-done = bf16[40,5120]{1,0:T(8,128)(2,1)} async-done(((bf16[320,5120]{1,0:T(8,128)(2,1)}), bf16[40,5120]{1,0:T(8,128)(2,1)}) %reduce-scatter.2.cloned.1.call-update) | async-done | bytes 409616 | tf_op jit(solution)/shard_map/reduce_scatter | solution.py:72
  238.1 2.2 fusion.23
  (24 shorter events, 0.4 us)
Async XLA Ops:
  6.5 66.2 %all-gather.8.cloned.1.call-start = ((), (), s32[]{:S(2)}) async-start(), calls=%async_computation.6 | async-start | bytes 1638400 | tf_op jit(solution)/shard_map/all_gather | solution.py:36
  25.8 37.0 %copy-start = (bf16[1,320,5120]{2,1,0:T(8,128)(2,1)S(1)}, bf16[1,320,5120]{2,1,0:T(8,128)(2,1)}, u32[]{:S(2)}) copy-start(bf16[1,320,5120]{2,1,0:T(8,128)(2,1)} %param.12) | copy-start | bytes 9830404
  25.8 47.0 %all-gather.10.cloned.1.call-start = ((), (), s32[]{:S(2)}) async-start(), calls=%async_computation.7 | async-start | bytes 1638400 | tf_op jit(solution)/shard_map/all_gather | solution.py:37
  40.9 78.4 %all-gather.12.cloned.1.call-start = ((), (), s32[]{:S(2)}) async-start(), calls=%async_computation.8 | async-start | bytes 2949120 | tf_op jit(solution)/shard_map/all_gather | solution.py:48
  41.6 95.8 %all-gather.6.cloned.1.call-start = ((), (), s32[]{:S(2)}) async-start(), calls=%async_computation.5 | async-start | bytes 1638400 | tf_op jit(solution)/shard_map/all_gather | solution.py:35
  42.8 28.7 %copy-start.3 = (s32[1,256]{1,0:T(1,128)S(1)}, s32[1,256]{1,0:T(1,128)}, u32[]{:S(2)}) copy-start(s32[1,256]{1,0:T(1,128)} %param.21) | copy-start | bytes 3076
  57.9 12.9 %all-to-all-start.3 = ((bf16[160,8,128]{2,0,1:T(8,128)(2,1)}), bf16[160,8,128]{2,0,1:T(8,128)(2,1)}, u32[]{:S(2)}, u32[]{:S(2)}) async-start(bf16[160,8,128]{2,0,1:T(8,128)(2,1)} %copy_bitcast_fusion), calls=%async_computation.3 | async-start | bytes 655360 | tf_op jit(solution)/shard_map/all_to_all | solution.py:32
  62.0 95.1 %all-gather.14.cloned.1.call-start = ((), (), s32[]{:S(2)}) async-start(), calls=%async_computation.9 | async-start | bytes 1638400 | tf_op jit(solution)/shard_map/all_gather | solution.py:38
  70.9 167.3 %reduce-scatter.2.cloned.1.call-start = ((), (), s32[]{:S(2)}) async-start(), calls=%async_computation.10 | async-start | bytes 3686400 | tf_op jit(solution)/shard_map/reduce_scatter | solution.py:72
  72.7 64.8 %copy-start.2 = (bf16[1,512,128]{2,1,0:T(8,128)(2,1)S(1)}, bf16[1,512,128]{2,1,0:T(8,128)(2,1)}, u32[]{:S(2)}) copy-start(bf16[1,512,128]{2,1,0:T(8,128)(2,1)} %param.18) | copy-start | bytes 393220
  123.7 33.4 %copy-start.1 = (bf16[1,512,128]{2,1,0:T(8,128)(2,1)S(1)}, bf16[1,512,128]{2,1,0:T(8,128)(2,1)}, u32[]{:S(2)}) copy-start(bf16[1,512,128]{2,1,0:T(8,128)(2,1)} %param.19) | copy-start | bytes 393220
Sparse Core Ops, SparseCore 0:
  25.9 16.5 all-gather.7
  44.1 18.1 all-gather.9
  64.5 54.6 all-gather.11
  120.6 16.7 all-gather.5
  138.9 18.1 all-gather.13
  162.0 76.1 reduce-scatter.1
where the time goes:
time: 248 us; the launch traced here: 247 us
  waiting for transfers between devices  155 us (62%)
  blocking collectives  45.1 us (18%)
  between operations  14.9 us (6%)
  other arithmetic  14.8 us (6%)
  matrix products  12.8 us (5%)
  starting transfers between devices  4.28 us (2%)
    reduce_scatter x1, waiting for transfers between devices, on_device(): lax.psum_scatter(lax.dot_general(attended, o_local, (((1,), (1,)), ((), (...  72.1 us
    all_gather x1, waiting for transfers between devices, on_device(): lax.all_gather(text_rows, 'tp', axis=1, tiled=True)  46.5 us
    all_to_all x1, blocking collectives, on_device(): lax.all_to_all(k_half, 'tp', split_axis=1, concat_axis=0, tiled=True)  18.1 us
    all_gather x1, waiting for transfers between devices, on_device(): lax.all_gather(o_block, 'req', axis=0, tiled=True)  14.7 us
    all_gather x1, waiting for transfers between devices, on_device(): lax.all_gather(q_block, 'req', axis=0, tiled=True)  13.8 us
    all_to_all x1, blocking collectives, on_device(): lax.all_to_all(v_half, 'tp', split_axis=1, concat_axis=0, tiled=True)  13.7 us
    all_to_all x1, blocking collectives, on_device(): lax.all_to_all(q_half, 'tp', split_axis=1, concat_axis=0, tiled=True)  13.2 us
    all_to_all x1, waiting for transfers between devices, on_device(): lax.all_to_all(o_half, 'tp', split_axis=1, concat_axis=0, tiled=True)  7.57 us
  transfers between devices with their start and end apart: 7, of which 5 were waited for; matrix products, arithmetic and copies ran while one was open for 8% of the time, Pallas kernels for 0%

commit v1 on v0

--- a/solution.py
+++ b/solution.py
@@ -25,8 +25,20 @@
     k_half = k_weight.astype(jnp.bfloat16)
     v_half = v_weight.astype(jnp.bfloat16)
     o_half = o_weight.astype(jnp.bfloat16)
+
+    def produce_streams(piece_in, along_dim, row_dim):
+        return jnp.concatenate(
+            lax.all_to_all(
+                jnp.stack(jnp.split(piece_in, lax.axis_size("tp"), axis=along_dim), axis=0),
+                "tp",
+                0,
+                0,
+            ),
+            row_dim,
+        )
+
     q_block, k_block, v_block, o_block = (
-        lax.all_to_all(q_half, "tp", split_axis=1, concat_axis=0, tiled=True),
+        produce_streams(q_half, 1, 0),
         lax.all_to_all(k_half, "tp", split_axis=1, concat_axis=0, tiled=True),
         lax.all_to_all(v_half, "tp", split_axis=1, concat_axis=0, tiled=True),
         lax.all_to_all(o_half, "tp", split_axis=1, concat_axis=0, tiled=True),

time: 248 us -> 248 us (level)
  no operation moved by 1% of the time
where the time goes in v1:
time: 248 us; the launch traced here: 247 us
  waiting for transfers between devices  155 us (62%)
  blocking collectives  45.1 us (18%)
  between operations  14.9 us (6%)
  other arithmetic  14.8 us (6%)
  matrix products  12.8 us (5%)
  starting transfers between devices  4.28 us (2%)
    reduce_scatter x1, waiting for transfers between devices, on_device(): lax.psum_scatter(lax.dot_general(attended, o_local, (((1,), (1,)), ((), (...  72.1 us
    all_gather x1, waiting for transfers between devices, on_device(): lax.all_gather(text_rows, 'tp', axis=1, tiled=True)  46.2 us
    all_to_all x1, blocking collectives, on_device(): lax.all_to_all(k_half, 'tp', split_axis=1, concat_axis=0, tiled=True)  18.1 us
    all_gather x1, waiting for transfers between devices, on_device(): lax.all_gather(o_block, 'req', axis=0, tiled=True)  14.7 us
    all_gather x1, waiting for transfers between devices, on_device(): lax.all_gather(q_block, 'req', axis=0, tiled=True)  13.8 us
    all_to_all x1, blocking collectives, on_device(): lax.all_to_all(v_half, 'tp', split_axis=1, concat_axis=0, tiled=True)  13.7 us
    all_to_all x1, blocking collectives, produce_streams(): lax.all_to_all(jnp.stack(jnp.split(piece_in, lax.axis_size('tp'), axis=al...  13.3 us
    all_to_all x1, waiting for transfers between devices, on_device(): lax.all_to_all(o_half, 'tp', split_axis=1, concat_axis=0, tiled=True)  7.59 us
  transfers between devices with their start and end apart: 7, of which 5 were waited for; matrix products, arithmetic and copies ran while one was open for 8% of the time, Pallas kernels for 0%

profile of v1, /device:TPU:0, one launch (start us, length us, event | category | flops | bytes accessed | tf_op | source)
XLA Modules:
  0.0 247.2 jit_solution(18000907425382071548)
XLA Ops:
  6.5 1.1 copy_bitcast_fusion.2
  7.7 18.1 %all_to_all.62 = bf16[160,8,128]{2,0,1:T(8,128)(2,1)} all-to-all(bf16[160,8,128]{2,0,1:T(8,128)(2,1)S(1)} %copy_bitcast_fusion.2), channel_id=1, replica_groups=mesh['req'=4,'tp'=8] {'tp'}, dimensions={1} | all-to-all | bytes 655360 | tf_op jit(solution)/shard_map/all_to_all | solution.py:42
  25.9 1.3 copy_bitcast_fusion.1
  27.1 13.7 %all_to_all.63 = bf16[160,8,128]{2,0,1:T(8,128)(2,1)} all-to-all(bf16[160,8,128]{2,0,1:T(8,128)(2,1)S(1)} %copy_bitcast_fusion.1), channel_id=1, replica_groups=mesh['req'=4,'tp'=8] {'tp'}, dimensions={1} | all-to-all | bytes 655360 | tf_op jit(solution)/shard_map/all_to_all | solution.py:43
  40.9 0.7 all-gather.12.cloned.1.call-update
  41.6 1.1 convert_element_type.51
  43.0 13.3 %all_to_all.64 = bf16[8,160,128]{2,1,0:T(8,128)(2,1)} all-to-all(bf16[8,160,128]{2,1,0:T(8,128)(2,1)S(1)} %fusion.35), channel_id=1, replica_groups=mesh['req'=4,'tp'=8] {'tp'}, dimensions={0} | all-to-all | bytes 655360 | tf_op jit(solution)/shard_map/all_to_all | solution.py:31
  56.3 1.9 copy_bitcast_fusion
  58.1 4.1 %all-to-all-start.3 = ((bf16[160,8,128]{2,0,1:T(8,128)(2,1)}), bf16[160,8,128]{2,0,1:T(8,128)(2,1)}, u32[]{:S(2)}, u32[]{:S(2)}) async-start(bf16[160,8,128]{2,0,1:T(8,128)(2,1)} %copy_bitcast_fusion), calls=%async_computation.3 | async-start | bytes 655360 | tf_op jit(solution)/shard_map/all_to_all | solution.py:44
  62.9 0.5 convert_reduce_fusion
  63.5 7.6 %all-to-all-done.3 = bf16[160,8,128]{2,0,1:T(8,128)(2,1)} async-done(((bf16[160,8,128]{2,0,1:T(8,128)(2,1)}), bf16[160,8,128]{2,0,1:T(8,128)(2,1)}, u32[]{:S(2)}, u32[]{:S(2)}) %all-to-all-start.3) | async-done | bytes 327712 | tf_op jit(solution)/shard_map/all_to_all | solution.py:44
  71.1 0.6 iota_compare_fusion.2
  71.7 0.2 fusion.22
  71.9 1.0 multiply_reduce_fusion
  73.0 46.2 %all-gather.12.cloned.1.call-done = bf16[1,256,5120]{2,1,0:T(8,128)(2,1)} async-done(((bf16[1,32,5120]{2,1,0:T(8,128)(2,1)}), bf16[1,256,5120]{2,1,0:T(8,128)(2,1)}) %all-gather.12.cloned.1.call-update) | async-done | bytes 2621456 | tf_op jit(solution)/shard_map/all_gather | solution.py:60
  119.2 4.4 %convolution_convert_fusion.1 = bf16[512,256]{1,0:T(8,128)(2,1)} fusion(bf16[1,256,5120]{2,1,0:T(8,128)(2,1)} %all-gather.12.cloned.1.call-done, bf16[5120,128]{1,0:T(8,128)(2,1)} %all-gather.10.cloned.1.call-done, bf16[5120,128]{1,0:T(8,128)(2,1)} %all-gather.8.cloned.1.call-done, s32[256]{0:T(256)S(1)} %bitcast.109), kind=kOutput, calls=%fused_computation.16 | convolution fusion | flops 743768064 | bytes 5506048 | tf_op jit(solution)/shard_map/dot_general | solution.py:67
  123.6 13.8 %all-gather.6.cloned.1.call-done = bf16[5120,128]{1,0:T(8,128)(2,1)} async-done(((bf16[1280,128]{1,0:T(8,128)(2,1)}), bf16[5120,128]{1,0:T(8,128)(2,1)}) %all-gather.6.cloned.1.call-update) | async-done | bytes 1310736 | tf_op jit(solution)/shard_map/all_gather | solution.py:47
  137.4 3.6 %fusion.45 = (f32[320]{0:T(512)S(1)}, f32[320,512]{1,0:T(8,128)}) fusion(bf16[512,256]{1,0:T(8,128)(2,1)} %convolution_convert_fusion.1, bf16[1,512,128]{2,1,0:T(8,128)(2,1)S(1)} %copy-done.2, pred[512]{0:T(512)(128)(4,1)S(1)} %fusion.22, bf16[5120,128]{1,0:T(8,128)(2,1)} %all-gather.6.cloned.1.call-done, bf16[1,320,5120]{2,1,0:T(8,128)(2,1)S(1)} %copy-done, ...), kind=kOutput, calls=%fused_computation.64 | convolution fusion | flops 470163136 | bytes 5530368 | tf_op jit(solution)/shard_map/dot_general | solution.py:72
  141.1 1.3 fusion.21
  142.4 14.7 %all-gather.14.cloned.1.call-done = bf16[5120,128]{1,0:T(8,128)(2,1)} async-done(((bf16[1280,128]{1,0:T(8,128)(2,1)}), bf16[5120,128]{1,0:T(8,128)(2,1)}) %all-gather.14.cloned.1.call-update) | async-done | bytes 1310736 | tf_op jit(solution)/shard_map/all_gather | solution.py:50
  157.1 4.8 %convolution_convert_fusion = bf16[320,5120]{1,0:T(8,128)(2,1)} fusion(bf16[5120,128]{1,0:T(8,128)(2,1)} %all-gather.14.cloned.1.call-done, f32[320,512]{1,0:T(8,128)} %get-tuple-element.6, f32[320]{0:T(512)S(1)} %fusion.21, f32[320]{0:T(512)S(1)} %get-tuple-element.5, bf16[512,256]{1,0:T(8,128)(2,1)} %convolution_convert_fusion.1, ...), kind=kOutput, calls=%fused_computation | convolution fusion | flops 463609856 | bytes 5508096 | tf_op jit(solution)/shard_map/dot_general | solution.py:85
  161.9 3.5 %convert_element_type.48 = f32[1,320,5120]{2,1,0:T(8,128)} convert(bf16[1,320,5120]{2,1,0:T(8,128)(2,1)S(1)} %copy-done) | non-fusion elementwise | flops 1638400 | bytes 9830400 | tf_op jit(solution)/shard_map/convert_element_type | solution.py:52
  166.0 72.1 %reduce-scatter.2.cloned.1.call-done = bf16[40,5120]{1,0:T(8,128)(2,1)} async-done(((bf16[320,5120]{1,0:T(8,128)(2,1)}), bf16[40,5120]{1,0:T(8,128)(2,1)}) %reduce-scatter.2.cloned.1.call-update) | async-done | bytes 409616 | tf_op jit(solution)/shard_map/reduce_scatter | solution.py:84
  238.1 2.2 fusion.23
  (32 shorter events, 0.5 us)
Async XLA Ops:
  6.5 66.4 %all-gather.8.cloned.1.call-start = ((), (), s32[]{:S(2)}) async-start(), calls=%async_computation.6 | async-start | bytes 1638400 | tf_op jit(solution)/shard_map/all_gather | solution.py:48
  25.8 37.1 %copy-start = (bf16[1,320,5120]{2,1,0:T(8,128)(2,1)S(1)}, bf16[1,320,5120]{2,1,0:T(8,128)(2,1)}, u32[]{:S(2)}) copy-start(bf16[1,320,5120]{2,1,0:T(8,128)(2,1)} %param.12) | copy-start | bytes 9830404
  25.8 47.2 %all-gather.10.cloned.1.call-start = ((), (), s32[]{:S(2)}) async-start(), calls=%async_computation.7 | async-start | bytes 1638400 | tf_op jit(solution)/shard_map/all_gather | solution.py:49
  40.9 78.4 %all-gather.12.cloned.1.call-start = ((), (), s32[]{:S(2)}) async-start(), calls=%async_computation.8 | async-start | bytes 2949120 | tf_op jit(solution)/shard_map/all_gather | solution.py:60
  41.6 95.8 %all-gather.6.cloned.1.call-start = ((), (), s32[]{:S(2)}) async-start(), calls=%async_computation.5 | async-start | bytes 1638400 | tf_op jit(solution)/shard_map/all_gather | solution.py:47
  42.9 28.8 %copy-start.3 = (s32[1,256]{1,0:T(1,128)S(1)}, s32[1,256]{1,0:T(1,128)}, u32[]{:S(2)}) copy-start(s32[1,256]{1,0:T(1,128)} %param.21) | copy-start | bytes 3076
  58.1 12.9 %all-to-all-start.3 = ((bf16[160,8,128]{2,0,1:T(8,128)(2,1)}), bf16[160,8,128]{2,0,1:T(8,128)(2,1)}, u32[]{:S(2)}, u32[]{:S(2)}) async-start(bf16[160,8,128]{2,0,1:T(8,128)(2,1)} %copy_bitcast_fusion), calls=%async_computation.3 | async-start | bytes 655360 | tf_op jit(solution)/shard_map/all_to_all | solution.py:44
  62.2 94.8 %all-gather.14.cloned.1.call-start = ((), (), s32[]{:S(2)}) async-start(), calls=%async_computation.9 | async-start | bytes 1638400 | tf_op jit(solution)/shard_map/all_gather | solution.py:50
  71.1 167.0 %reduce-scatter.2.cloned.1.call-start = ((), (), s32[]{:S(2)}) async-start(), calls=%async_computation.10 | async-start | bytes 3686400 | tf_op jit(solution)/shard_map/reduce_scatter | solution.py:84
  72.9 64.5 %copy-start.2 = (bf16[1,512,128]{2,1,0:T(8,128)(2,1)S(1)}, bf16[1,512,128]{2,1,0:T(8,128)(2,1)}, u32[]{:S(2)}) copy-start(bf16[1,512,128]{2,1,0:T(8,128)(2,1)} %param.18) | copy-start | bytes 393220
  123.6 33.4 %copy-start.1 = (bf16[1,512,128]{2,1,0:T(8,128)(2,1)S(1)}, bf16[1,512,128]{2,1,0:T(8,128)(2,1)}, u32[]{:S(2)}) copy-start(bf16[1,512,128]{2,1,0:T(8,128)(2,1)} %param.19) | copy-start | bytes 393220
Sparse Core Ops, SparseCore 0:
  25.9 16.5 all-gather.7
  44.1 18.1 all-gather.9
  64.5 54.6 all-gather.11
  120.6 16.7 all-gather.5
  138.8 18.1 all-gather.13
  162.0 76.1 reduce-scatter.1
